TPU v7x, 128 devices: a whole 4x4x4 slice. The times are simulated.
128 devices in a mesh: rows: 32 (over y, z, core), cols: 4 (over x).
Axes of the slice: x: 4, y: 4, z: 4, core: 2. Of those that a mesh axis runs over, the one named last changes fastest.
Arguments:
- points: float32 [16, 1048576], P(None, ('rows', 'cols')), may hold values from -2 to 2
- coeffs: float32 [32, 1048576], P(None, ('rows', 'cols')), may hold values from -6 to 6
- velocity: float32 [32, 1048576], P(None, ('rows', 'cols')), may hold values from -4 to 4
- targets: float32 [32, 1048576], P(None, ('rows', 'cols')), may hold values from -6 to 6
- batch_index: int32 [2, 2048], replicated, may hold values from 0 to 1048575, as said below
- test_points: float32 [16, 4096], P(None, 'cols'), may hold values from -2 to 2
Outputs:
- coeffs_out: float32 [32, 1048576], P(None, ('rows', 'cols'))
- velocity_out: float32 [32, 1048576], P(None, ('rows', 'cols'))
- samples: float32 [32, 4096], P(None, 'cols')
Inputs may be any that keep to these rules, and one draw needn't show every extreme that they name: `batch_index`: row numbers of training points, 2048 in each step; a row may repeat within a step, and rows of low-numbered devices are drawn far more often than others.
All inputs are finite; a program needn't handle non-finite values.
Results may differ from a plain program's by a relative error of at most 0.0042.
Values sent between devices are 32-bit elements; how exact they have to be, the bound alone decides.
No kernel may reach another device: no remote copies, remote signals or barrier semaphores. Data moves between devices by JAX's collectives and lax.ppermute only.
A program may use at most 128 MiB of HBM per device.

v0:
```python
import math
import jax
import jax.numpy as jnp
from jax import lax
from jax.sharding import PartitionSpec as P

SCALE = 3.0**0.5 / 1.25


def matern_tile(points_block, queries):
    cross_term = jnp.dot(
        points_block.T, queries, precision=lax.Precision.HIGHEST, preferred_element_type=jnp.float32
    )
    sq_points = jnp.sum(points_block * points_block, axis=0)
    sq_queries = jnp.sum(queries * queries, axis=0)
    dist_sq = jnp.maximum(sq_points[:, None] + sq_queries[None, :] - 2.0 * cross_term, 0.0)
    scaled = SCALE * jnp.sqrt(dist_sq)
    return ((1.0 + scaled) * jnp.exp(-scaled)).astype(jnp.bfloat16)


def kernel_times(points, coeff_half, queries):
    query_count = queries.shape[1]
    blk_width = math.gcd(query_count, 512)
    blocks = queries.reshape(queries.shape[0], query_count // blk_width, blk_width).transpose(
        1, 0, 2
    )

    def apply_block(block):
        return jnp.dot(coeff_half, matern_tile(points, block), preferred_element_type=jnp.float32)

    results = lax.map(apply_block, blocks)
    return results.transpose(1, 0, 2).reshape(coeff_half.shape[0], query_count)


def per_device(points, coeffs, velocity, targets, batch_index, test_points):
    local_count = points.shape[1]
    row_start = lax.axis_index(("rows", "cols")) * local_count

    def take_owned(array, safe_rows, weights):
        return jnp.take(array, safe_rows, axis=1) * weights[None, :]

    steps_total = batch_index.shape[0]
    coeffs_now = coeffs
    velocity_now = velocity
    for step_no in range(steps_total):
        picked = batch_index[step_no]
        offset = picked - row_start
        inside = (offset >= 0) & (offset < local_count)
        owned_safe_rows = jnp.clip(offset, 0, local_count - 1)
        safe_rows = owned_safe_rows
        weights = inside.astype(jnp.float32)
        batch_points = lax.psum(take_owned(points, safe_rows, weights), ("rows", "cols"))
        partial_sums = kernel_times(points, coeffs_now.astype(jnp.bfloat16), batch_points)
        own_terms = take_owned(coeffs_now, safe_rows, weights) * 1.0 - take_owned(
            targets, safe_rows, weights
        )
        gradient = lax.psum(partial_sums + own_terms, ("rows", "cols"))
        summed = jnp.zeros_like(coeffs_now).at[:, safe_rows].add(gradient * weights[None, :])
        velocity_now = 0.9 * velocity_now - 0.5 * summed
        coeffs_now = coeffs_now + velocity_now
    coeff_half = coeffs_now.astype(jnp.bfloat16)
    partial_test = kernel_times(
        points, coeff_half, lax.all_gather(test_points, "cols", axis=1, tiled=True)
    )
    slab_sum = lax.psum_scatter(partial_test, "cols", scatter_dimension=1, tiled=True)
    slab_sum = lax.psum(slab_sum, "rows")
    return (coeffs_now, velocity_now, slab_sum)


def solution(mesh):
    return jax.shard_map(
        per_device,
        mesh=mesh,
        in_specs=(
            P(None, ("rows", "cols")),
            P(None, ("rows", "cols")),
            P(None, ("rows", "cols")),
            P(None, ("rows", "cols")),
            P(),
            P(None, "cols"),
        ),
        out_specs=(P(None, ("rows", "cols")), P(None, ("rows", "cols")), P(None, "cols")),
        check_vma=False,
    )
```

profile of v0, /device:TPU:1, one launch (start us, length us, event | category | flops | bytes accessed | tf_op | source)
XLA Modules:
  0.0 1088.0 jit_solution(15402246799207417307)
XLA Ops:
  25.7 9.8 gather_fusion.3
  43.7 9.8 gather_fusion.2
  53.6 9.8 gather_fusion.1
  64.4 104.7 %all-reduce.6.cloned.1.call-done = f32[4,16,512]{2,1,0:T(8,128)} async-done(((f32[4,16,512]{2,1,0:T(8,128)}), f32[4,16,512]{2,1,0:T(8,128)}) %all-reduce.6.cloned.1.call-update) | async-done | bytes 131088 | tf_op jit(solution)/shard_map/psum | solution.py:52
  169.1 109.0 %while.36 = (s32[]{:T(128)}, f32[4,32,512]{2,1,0:T(8,128)S(1)}, f32[8192]{0:T(1024)S(1)}, f32[4,16,512]{2,1,0:T(8,128)}, f32[16,8192]{1,0:T(8,128)S(1)}, /*index=5*/bf16[32,8192]{1,0:T(8,128)(2,1)S(1)}, s32[]{:T(128)}) while((s32[]{:T(128)}, f32[4,32,512]{2,1,0:T(8,128)S(1)}, f32[8192]{0:T(1024)S(1)}, f32[4,16,512]{2,1,0:T(8,128)}, ...), condition=%wide.region_4.6_spmd, body=%wide.region_2.5_spmd.sunk | while | flops 1111506432 | bytes 17993824 | solution.py:31
  170.0 23.8 %multiply_convert_fusion.6 = bf16[8192,512]{0,1:T(8,128)(2,1)S(1)} fusion(f32[16,8192]{1,0:T(8,128)S(1)} %get-tuple-element.416, f32[512]{0:T(512)S(1)} %fusion.69, f32[8192]{0:T(1024)S(1)} %get-tuple-element.414, f32[4,16,512]{2,1,0:T(8,128)} %get-tuple-element.415, s32[]{:T(128)S(6)} %copy.59), kind=kOutput, calls=%fused_computation.12.clone.1 | convolution fusion | flops 843055104 | bytes 8980484 | tf_op jit(solution)/shard_map/while/body/eval_jaxpr/dot_general | solution.py:11
  197.2 23.8 %multiply_convert_fusion.6 = bf16[8192,512]{0,1:T(8,128)(2,1)S(1)} fusion(f32[16,8192]{1,0:T(8,128)S(1)} %get-tuple-element.416, f32[512]{0:T(512)S(1)} %fusion.69, f32[8192]{0:T(1024)S(1)} %get-tuple-element.414, f32[4,16,512]{2,1,0:T(8,128)} %get-tuple-element.415, s32[]{:T(128)S(6)} %copy.59), kind=kOutput, calls=%fused_computation.12.clone.1 | convolution fusion | flops 843055104 | bytes 8980484 | tf_op jit(solution)/shard_map/while/body/eval_jaxpr/dot_general | solution.py:11
  224.4 23.8 %multiply_convert_fusion.6 = bf16[8192,512]{0,1:T(8,128)(2,1)S(1)} fusion(f32[16,8192]{1,0:T(8,128)S(1)} %get-tuple-element.416, f32[512]{0:T(512)S(1)} %fusion.69, f32[8192]{0:T(1024)S(1)} %get-tuple-element.414, f32[4,16,512]{2,1,0:T(8,128)} %get-tuple-element.415, s32[]{:T(128)S(6)} %copy.59), kind=kOutput, calls=%fused_computation.12.clone.1 | convolution fusion | flops 843055104 | bytes 8980484 | tf_op jit(solution)/shard_map/while/body/eval_jaxpr/dot_general | solution.py:11
  251.6 23.8 %multiply_convert_fusion.6 = bf16[8192,512]{0,1:T(8,128)(2,1)S(1)} fusion(f32[16,8192]{1,0:T(8,128)S(1)} %get-tuple-element.416, f32[512]{0:T(512)S(1)} %fusion.69, f32[8192]{0:T(1024)S(1)} %get-tuple-element.414, f32[4,16,512]{2,1,0:T(8,128)} %get-tuple-element.415, s32[]{:T(128)S(6)} %copy.59), kind=kOutput, calls=%fused_computation.12.clone.1 | convolution fusion | flops 843055104 | bytes 8980484 | tf_op jit(solution)/shard_map/while/body/eval_jaxpr/dot_general | solution.py:11
  294.7 131.7 %all-reduce.12.cloned.1.call-done = (f32[32,2048]{0,1:T(8,128)}, f32[4,16,512]{2,1,0:T(8,128)}) async-done(((f32[32,2048]{0,1:T(8,128)}, f32[4,16,512]{2,1,0:T(8,128)}), (f32[32,2048]{0,1:T(8,128)}, f32[4,16,512]{2,1,0:T(8,128)})) %all-reduce.12.cloned.1.call-update) | async-done | bytes 393232 | tf_op jit(solution)/shard_map/psum | solution.py:57
  426.4 15.7 %scatter_custom_fusion = f32[32,8192]{0,1:T(8,128)} fusion(s32[2048]{0:T(1024)S(1)} %bitcast.194, f32[]{:T(128)} %constant.138.clone.1, f32[32,2048]{0,1:T(8,128)} %get-tuple-element.272, f32[2048]{0:T(1024)S(1)} %bitcast.188), kind=kCustom, calls=%fused_computation.46 | custom fusion | flops 131072 | bytes 1318916 | tf_op jit(solution)/shard_map/scatter-add | solution.py:58
  450.4 102.8 %while.37 = (s32[]{:T(128)}, f32[4,32,512]{2,1,0:T(8,128)S(1)}, f32[8192]{0:T(1024)S(1)}, f32[4,16,512]{2,1,0:T(8,128)S(1)}, f32[16,8192]{1,0:T(8,128)S(1)}, /*index=5*/bf16[32,8192]{1,0:T(8,128)(2,1)S(1)}, s32[]{:T(128)}) while((s32[]{:T(128)}, f32[4,32,512]{2,1,0:T(8,128)S(1)}, f32[8192]{0:T(1024)S(1)}, f32[4,16,512]{2,1,0:T(8,128)S(1)}, ...), condition=%wide.region_10.13_spmd, body=%wide.region_8.12_spmd.sunk | while | flops 1111506432 | bytes 17993824 | solution.py:31
  450.4 23.0 %multiply_convert_fusion.7 = bf16[8192,512]{0,1:T(8,128)(2,1)S(1)} fusion(f32[16,8192]{1,0:T(8,128)S(1)} %get-tuple-element.437, f32[512]{0:T(512)S(1)} %fusion.75, f32[8192]{0:T(1024)S(1)} %get-tuple-element.435, f32[4,16,512]{2,1,0:T(8,128)S(1)} %get-tuple-element.436, s32[]{:T(128)S(6)} %copy.67), kind=kOutput, calls=%fused_computation.24.clone.1 | convolution fusion | flops 843055104 | bytes 8980484 | tf_op jit(solution)/shard_map/while/body/eval_jaxpr/dot_general | solution.py:11
  476.1 23.1 %multiply_convert_fusion.7 = bf16[8192,512]{0,1:T(8,128)(2,1)S(1)} fusion(f32[16,8192]{1,0:T(8,128)S(1)} %get-tuple-element.437, f32[512]{0:T(512)S(1)} %fusion.75, f32[8192]{0:T(1024)S(1)} %get-tuple-element.435, f32[4,16,512]{2,1,0:T(8,128)S(1)} %get-tuple-element.436, s32[]{:T(128)S(6)} %copy.67), kind=kOutput, calls=%fused_computation.24.clone.1 | convolution fusion | flops 843055104 | bytes 8980484 | tf_op jit(solution)/shard_map/while/body/eval_jaxpr/dot_general | solution.py:11
  501.8 23.1 %multiply_convert_fusion.7 = bf16[8192,512]{0,1:T(8,128)(2,1)S(1)} fusion(f32[16,8192]{1,0:T(8,128)S(1)} %get-tuple-element.437, f32[512]{0:T(512)S(1)} %fusion.75, f32[8192]{0:T(1024)S(1)} %get-tuple-element.435, f32[4,16,512]{2,1,0:T(8,128)S(1)} %get-tuple-element.436, s32[]{:T(128)S(6)} %copy.67), kind=kOutput, calls=%fused_computation.24.clone.1 | convolution fusion | flops 843055104 | bytes 8980484 | tf_op jit(solution)/shard_map/while/body/eval_jaxpr/dot_general | solution.py:11
  527.5 23.1 %multiply_convert_fusion.7 = bf16[8192,512]{0,1:T(8,128)(2,1)S(1)} fusion(f32[16,8192]{1,0:T(8,128)S(1)} %get-tuple-element.437, f32[512]{0:T(512)S(1)} %fusion.75, f32[8192]{0:T(1024)S(1)} %get-tuple-element.435, f32[4,16,512]{2,1,0:T(8,128)S(1)} %get-tuple-element.436, s32[]{:T(128)S(6)} %copy.67), kind=kOutput, calls=%fused_computation.24.clone.1 | convolution fusion | flops 843055104 | bytes 8980484 | tf_op jit(solution)/shard_map/while/body/eval_jaxpr/dot_general | solution.py:11
  553.5 9.8 gather_fusion.4
  566.0 10.1 all_gather.3
  576.3 138.1 %all-reduce.8.cloned.1.call-done = f32[32,2048]{0,1:T(8,128)} async-done(((f32[32,2048]{0,1:T(8,128)}), f32[32,2048]{0,1:T(8,128)}) %all-reduce.8.cloned.1.call-update) | async-done | bytes 262160 | tf_op jit(solution)/shard_map/psum | solution.py:57
  714.3 15.7 %scatter_custom_fusion.1 = f32[32,8192]{0,1:T(8,128)} fusion(s32[2048]{0:T(1024)} %bitcast.193, f32[]{:T(128)} %constant.138.clone.1, f32[32,2048]{0,1:T(8,128)} %all-reduce.8.cloned.1.call-done, f32[2048]{0:T(1024)S(1)} %bitcast.185), kind=kCustom, calls=%fused_computation.44 | custom fusion | flops 131072 | bytes 2105856 | tf_op jit(solution)/shard_map/scatter-add | solution.py:58
  730.0 10.3 fusion.37
  741.1 210.8 %while.38 = (s32[]{:T(128)}, f32[8,32,512]{2,1,0:T(8,128)}, f32[8192]{0:T(1024)S(1)}, f32[8,16,512]{2,0,1:T(8,128)S(1)}, f32[16,8192]{1,0:T(8,128)S(1)}, /*index=5*/bf16[32,8192]{1,0:T(8,128)(2,1)S(1)}, s32[]{:T(128)}) while((s32[]{:T(128)}, f32[8,32,512]{2,1,0:T(8,128)}, f32[8192]{0:T(1024)S(1)}, f32[8,16,512]{2,0,1:T(8,128)S(1)}, ...), condition=%wide.region_15.18_spmd, body=%wide.region_13.17_spmd.sunk | while | flops 1111506432 | bytes 18059356 | solution.py:31
  741.2 23.0 %multiply_convert_fusion.8 = bf16[8192,512]{0,1:T(8,128)(2,1)S(1)} fusion(f32[16,8192]{1,0:T(8,128)S(1)} %get-tuple-element.458, f32[512]{0:T(512)S(1)} %multiply_reduce_fusion.3, f32[8192]{0:T(1024)S(1)} %get-tuple-element.456, f32[1,16,512]{2,0,1:T(1,128)S(1)} %constant_dynamic-slice_fusion.2), kind=kOutput, calls=%fused_computation.36.clone.1 | convolution fusion | flops 843055104 | bytes 8980480 | tf_op jit(solution)/shard_map/while/body/eval_jaxpr/dot_general | solution.py:11
  767.5 23.0 %multiply_convert_fusion.8 = bf16[8192,512]{0,1:T(8,128)(2,1)S(1)} fusion(f32[16,8192]{1,0:T(8,128)S(1)} %get-tuple-element.458, f32[512]{0:T(512)S(1)} %multiply_reduce_fusion.3, f32[8192]{0:T(1024)S(1)} %get-tuple-element.456, f32[1,16,512]{2,0,1:T(1,128)S(1)} %constant_dynamic-slice_fusion.2), kind=kOutput, calls=%fused_computation.36.clone.1 | convolution fusion | flops 843055104 | bytes 8980480 | tf_op jit(solution)/shard_map/while/body/eval_jaxpr/dot_general | solution.py:11
  793.9 23.0 %multiply_convert_fusion.8 = bf16[8192,512]{0,1:T(8,128)(2,1)S(1)} fusion(f32[16,8192]{1,0:T(8,128)S(1)} %get-tuple-element.458, f32[512]{0:T(512)S(1)} %multiply_reduce_fusion.3, f32[8192]{0:T(1024)S(1)} %get-tuple-element.456, f32[1,16,512]{2,0,1:T(1,128)S(1)} %constant_dynamic-slice_fusion.2), kind=kOutput, calls=%fused_computation.36.clone.1 | convolution fusion | flops 843055104 | bytes 8980480 | tf_op jit(solution)/shard_map/while/body/eval_jaxpr/dot_general | solution.py:11
  820.2 23.0 %multiply_convert_fusion.8 = bf16[8192,512]{0,1:T(8,128)(2,1)S(1)} fusion(f32[16,8192]{1,0:T(8,128)S(1)} %get-tuple-element.458, f32[512]{0:T(512)S(1)} %multiply_reduce_fusion.3, f32[8192]{0:T(1024)S(1)} %get-tuple-element.456, f32[1,16,512]{2,0,1:T(1,128)S(1)} %constant_dynamic-slice_fusion.2), kind=kOutput, calls=%fused_computation.36.clone.1 | convolution fusion | flops 843055104 | bytes 8980480 | tf_op jit(solution)/shard_map/while/body/eval_jaxpr/dot_general | solution.py:11
  846.6 23.0 %multiply_convert_fusion.8 = bf16[8192,512]{0,1:T(8,128)(2,1)S(1)} fusion(f32[16,8192]{1,0:T(8,128)S(1)} %get-tuple-element.458, f32[512]{0:T(512)S(1)} %multiply_reduce_fusion.3, f32[8192]{0:T(1024)S(1)} %get-tuple-element.456, f32[1,16,512]{2,0,1:T(1,128)S(1)} %constant_dynamic-slice_fusion.2), kind=kOutput, calls=%fused_computation.36.clone.1 | convolution fusion | flops 843055104 | bytes 8980480 | tf_op jit(solution)/shard_map/while/body/eval_jaxpr/dot_general | solution.py:11
  872.9 23.0 %multiply_convert_fusion.8 = bf16[8192,512]{0,1:T(8,128)(2,1)S(1)} fusion(f32[16,8192]{1,0:T(8,128)S(1)} %get-tuple-element.458, f32[512]{0:T(512)S(1)} %multiply_reduce_fusion.3, f32[8192]{0:T(1024)S(1)} %get-tuple-element.456, f32[1,16,512]{2,0,1:T(1,128)S(1)} %constant_dynamic-slice_fusion.2), kind=kOutput, calls=%fused_computation.36.clone.1 | convolution fusion | flops 843055104 | bytes 8980480 | tf_op jit(solution)/shard_map/while/body/eval_jaxpr/dot_general | solution.py:11
  899.3 23.0 %multiply_convert_fusion.8 = bf16[8192,512]{0,1:T(8,128)(2,1)S(1)} fusion(f32[16,8192]{1,0:T(8,128)S(1)} %get-tuple-element.458, f32[512]{0:T(512)S(1)} %multiply_reduce_fusion.3, f32[8192]{0:T(1024)S(1)} %get-tuple-element.456, f32[1,16,512]{2,0,1:T(1,128)S(1)} %constant_dynamic-slice_fusion.2), kind=kOutput, calls=%fused_computation.36.clone.1 | convolution fusion | flops 843055104 | bytes 8980480 | tf_op jit(solution)/shard_map/while/body/eval_jaxpr/dot_general | solution.py:11
  925.6 23.0 %multiply_convert_fusion.8 = bf16[8192,512]{0,1:T(8,128)(2,1)S(1)} fusion(f32[16,8192]{1,0:T(8,128)S(1)} %get-tuple-element.458, f32[512]{0:T(512)S(1)} %multiply_reduce_fusion.3, f32[8192]{0:T(1024)S(1)} %get-tuple-element.456, f32[1,16,512]{2,0,1:T(1,128)S(1)} %constant_dynamic-slice_fusion.2), kind=kOutput, calls=%fused_computation.36.clone.1 | convolution fusion | flops 843055104 | bytes 8980480 | tf_op jit(solution)/shard_map/while/body/eval_jaxpr/dot_general | solution.py:11
  953.8 21.0 %reduce-scatter.2.cloned.1.call-done = f32[32,1024]{1,0:T(8,128)} async-done(((f32[32,4096]{1,0:T(8,128)}), f32[32,1024]{1,0:T(8,128)}) %reduce-scatter.2.cloned.1.call-update) | async-done | bytes 131088 | tf_op jit(solution)/shard_map/reduce_scatter | solution.py:65
  982.0 97.5 %all-reduce.10.cloned.1.call-done = f32[32,1024]{1,0:T(8,128)} async-done(((f32[32,1024]{1,0:T(8,128)}), f32[32,1024]{1,0:T(8,128)}) %all-reduce.10.cloned.1.call-update) | async-done | bytes 131088 | tf_op jit(solution)/shard_map/psum | solution.py:66
  (103 shorter events, 117.7 us)
Async XLA Ops:
  7.2 30.1 %copy-start.1 = (f32[16,8192]{1,0:T(8,128)S(1)}, f32[16,8192]{1,0:T(8,128)}, u32[]{:S(2)}) copy-start(f32[16,8192]{1,0:T(8,128)} %param.16) | copy-start | bytes 1572868
  7.2 30.2 %copy-start = (f32[32,8192]{1,0:T(8,128)S(1)}, f32[32,8192]{1,0:T(8,128)}, u32[]{:S(2)}) copy-start(f32[32,8192]{1,0:T(8,128)} %param.17) | copy-start | bytes 3145732
  7.2 161.9 %all-reduce.6.cloned.1.call-start = ((), (), s32[]{:S(2)}) async-start(), calls=%async_computation.1 | async-start | bytes 262144 | tf_op jit(solution)/shard_map/psum | solution.py:52
  8.1 29.2 %copy-start.5 = (f32[1,2048]{1,0:T(1,128)}, f32[1,2048]{1,0:T(1,128)S(1)}, u32[]{:S(2)}) copy-start(f32[1,2048]{1,0:T(1,128)S(1)} %get-tuple-element.283) | copy-start | bytes 24580
  25.6 400.7 %all-reduce.12.cloned.1.call-start = ((), (), s32[]{:S(2)}) async-start(), calls=%async_computation.5 | async-start | bytes 2359296 | tf_op jit(solution)/shard_map/psum | solution.py:57
  25.7 27.9 %copy-start.8 = (pred[2048]{0:T(1024)(128)(4,1)}, pred[2048]{0:T(1024)(128)(4,1)S(1)}, u32[]{:S(2)}) copy-start(pred[2048]{0:T(1024)(128)(4,1)S(1)} %compare_and_fusion) | copy-start | bytes 6148
  169.1 109.3 %copy-start.3 = (f32[2048,32]{1,0:T(8,128)S(1)}, f32[2048,32]{1,0:T(8,128)}, u32[]{:S(2)}) copy-start(f32[2048,32]{1,0:T(8,128)} %gather_fusion.2) | copy-start | bytes 786436
  281.0 433.3 %all-reduce.8.cloned.1.call-start = ((), (), s32[]{:S(2)}) async-start(), calls=%async_computation.2 | async-start | bytes 2097152 | tf_op jit(solution)/shard_map/psum | solution.py:57
  442.1 8.3 copy-start.4
  450.4 113.0 %copy-start.2 = (f32[2048,32]{1,0:T(8,128)S(1)}, f32[2048,32]{1,0:T(8,128)}, u32[]{:S(2)}) copy-start(f32[2048,32]{1,0:T(8,128)} %gather_fusion.5) | copy-start | bytes 786436
  450.4 113.0 %copy-start.6 = (f32[1,2048]{1,0:T(1,128)S(1)}, f32[1,2048]{1,0:T(1,128)}, u32[]{:S(2)}) copy-start(f32[1,2048]{1,0:T(1,128)} %copy-done.5) | copy-start | bytes 24580
  450.4 113.0 %copy-start.9 = (pred[2048]{0:T(1024)(128)(4,1)S(1)}, pred[2048]{0:T(1024)(128)(4,1)}, u32[]{:S(2)}) copy-start(pred[2048]{0:T(1024)(128)(4,1)} %copy-done.8) | copy-start | bytes 6148
  553.2 12.9 %copy-start.7 = (f32[16,1024]{1,0:T(8,128)S(1)}, f32[16,1024]{1,0:T(8,128)}, u32[]{:S(2)}) copy-start(f32[16,1024]{1,0:T(8,128)} %param.21) | copy-start | bytes 196612
  566.0 408.8 %reduce-scatter.2.cloned.1.call-start = ((), (), s32[]{:S(2)}) async-start(), calls=%async_computation.3 | async-start | bytes 655360 | tf_op jit(solution)/shard_map/reduce_scatter | solution.py:65
  953.8 125.7 %all-reduce.10.cloned.1.call-start = ((), (), s32[]{:S(2)}) async-start(), calls=%async_computation.4 | async-start | bytes 262144 | tf_op jit(solution)/shard_map/psum | solution.py:66
Sparse Core Ops, SparseCore 0:
  25.7 143.2 all-reduce.5
  281.2 145.1 all-reduce.11
  566.1 148.1 all-reduce.7
  953.9 20.8 reduce-scatter.1
  978.2 101.2 all-reduce.9
where the time goes:
time: 1100 us; the launch traced here: 1090 us
  waiting for transfers between devices  493 us (45%)
  matrix products  419 us (38%)
  local copies, waits for them, and re-layouts  87.6 us (8%)
  other arithmetic  63.8 us (6%)
  between operations  14.4 us (1%)
    dot_general x16, matrix products, matern_tile(): jnp.dot(points_block.T, queries, precision=lax.Precision.HIGHEST, preferr...  372 us
    psum x2, waiting for transfers between devices, per_device(): gradient = lax.psum(partial_sums + own_terms, ('rows', 'cols'))  270 us
    psum x1, waiting for transfers between devices, per_device(): lax.psum(take_owned(points, safe_rows, weights), ('rows', 'cols'))  105 us
    psum x1, waiting for transfers between devices, per_device(): slab_sum = lax.psum(slab_sum, 'rows')  97.5 us
    gather x6, local copies, waits for them, and re-layouts, take_owned(): return jnp.take(array, safe_rows, axis=1) * weights[None, :]  58.9 us
    dot_general x16, matrix products, apply_block(): jnp.dot(coeff_half, matern_tile(points, block), preferred_element_type=jn...  46.8 us
    scatter-add x2, other arithmetic, per_device(): jnp.zeros_like(coeffs_now).at[:, safe_rows].add(gradient * weights[None, :])  31.4 us
    unnamed x28, local copies, waits for them, and re-layouts  22.4 us
  transfers between devices with their start and end apart: 5, of which 5 were waited for; matrix products, arithmetic and copies ran while one was open for 5% of the time, Pallas kernels for 0%

commit v1 on v0

--- a/solution.py
+++ b/solution.py
@@ -49,7 +49,9 @@
         owned_safe_rows = jnp.clip(offset, 0, local_count - 1)
         safe_rows = owned_safe_rows
         weights = inside.astype(jnp.float32)
-        batch_points = lax.psum(take_owned(points, safe_rows, weights), ("rows", "cols"))
+        batch_points = jnp.sum(
+            lax.all_gather(take_owned(points, safe_rows, weights), ("rows", "cols")), axis=0
+        )
         partial_sums = kernel_times(points, coeffs_now.astype(jnp.bfloat16), batch_points)
         own_terms = take_owned(coeffs_now, safe_rows, weights) * 1.0 - take_owned(
             targets, safe_rows, weights

time: 1100 us -> 1040 us (0.945)
  waiting for transfers between devices: 493 us -> 423 us
  starting transfers between devices: 0.38 us -> 11.8 us
    psum x1 -> x0, waiting for transfers between devices: 105 us -> none  [per_device(): lax.psum(take_owned(points, safe_rows, weights), ('rows', 'cols'))]
    all_gather x0 -> x2, waiting for transfers between devices: none -> 51.3 us  [per_device(): lax.all_gather(take_owned(points, safe_rows, weights), ('rows', 'cols'))]
    psum x2, waiting for transfers between devices: 270 us -> 254 us  [per_device(): gradient = lax.psum(partial_sums + own_terms, ('rows', 'cols'))]
    reduce_sum x0 -> x2, other arithmetic: none -> 13.2 us  [per_device(): jnp.sum(lax.all_gather(take_owned(points, safe_rows, weights), ('rows', '...]
    psum x2, starting transfers between devices: 0.26 us -> 11.6 us  [per_device(): gradient = lax.psum(partial_sums + own_terms, ('rows', 'cols'))]
    gather x6 -> x8, local copies, waits for them, and re-layouts: 58.9 us -> 53 us  [take_owned(): return jnp.take(array, safe_rows, axis=1) * weights[None, :]]
    unnamed x28 -> x24, local copies, waits for them, and re-layouts: 22.4 us -> 22.4 us
  transfers between devices with their start and end apart: 5 -> 6, of which waited for: 5 -> 5; matrix products, arithmetic and copies ran while one was open for 5% -> 17% of each run, Pallas kernels for 0% -> 0%
where the time goes in v1:
time: 1040 us; the launch traced here: 1030 us
  waiting for transfers between devices  423 us (41%)
  matrix products  415 us (40%)
  local copies, waits for them, and re-layouts  80.3 us (8%)
  other arithmetic  71.8 us (7%)
  between operations  14.7 us (1%)
  starting transfers between devices  11.8 us (1%)
    dot_general x16, matrix products, matern_tile(): jnp.dot(points_block.T, queries, precision=lax.Precision.HIGHEST, preferr...  369 us
    psum x2, waiting for transfers between devices, per_device(): gradient = lax.psum(partial_sums + own_terms, ('rows', 'cols'))  254 us
    psum x1, waiting for transfers between devices, per_device(): slab_sum = lax.psum(slab_sum, 'rows')  97.2 us
    gather x8, local copies, waits for them, and re-layouts, take_owned(): return jnp.take(array, safe_rows, axis=1) * weights[None, :]  53 us
    all_gather x2, waiting for transfers between devices, per_device(): lax.all_gather(take_owned(points, safe_rows, weights), ('rows', 'cols'))  51.3 us
    dot_general x16, matrix products, apply_block(): jnp.dot(coeff_half, matern_tile(points, block), preferred_element_type=jn...  46.8 us
    scatter-add x2, other arithmetic, per_device(): jnp.zeros_like(coeffs_now).at[:, safe_rows].add(gradient * weights[None, :])  31.4 us
    unnamed x24, local copies, waits for them, and re-layouts  22.4 us
  transfers between devices with their start and end apart: 6, of which 5 were waited for; matrix products, arithmetic and copies ran while one was open for 17% of the time, Pallas kernels for 0%

profile of v1, /device:TPU:1, one launch (start us, length us, event | category | flops | bytes accessed | tf_op | source)
XLA Modules:
  0.0 1026.8 jit_solution(1262902991214102936)
XLA Ops:
  44.6 9.8 gather_fusion.1
  54.5 51.3 %all-gather.5.cloned.1.call-done = f32[2048,2048]{1,0:T(8,128)} async-done(((f32[16,2048]{1,0:T(8,128)}), f32[2048,2048]{1,0:T(8,128)}) %all-gather.5.cloned.1.call-update) | async-done | bytes 16777232 | tf_op jit(solution)/shard_map/all_gather | solution.py:53
  112.5 102.9 %while.36 = (s32[]{:T(128)}, f32[4,32,512]{2,1,0:T(8,128)S(1)}, f32[8192]{0:T(1024)S(1)}, f32[4,16,512]{2,0,1:T(4,128)S(1)}, f32[16,8192]{1,0:T(8,128)S(1)}, /*index=5*/bf16[32,8192]{1,0:T(8,128)(2,1)S(1)}, s32[]{:T(128)}) while((s32[]{:T(128)}, f32[4,32,512]{2,1,0:T(8,128)S(1)}, f32[8192]{0:T(1024)S(1)}, f32[4,16,512]{2,0,1:T(4,128)S(1)}, ...), condition=%wide.region_4.6_spmd, body=%wide.region_2.5_spmd.sunk | while | flops 1111506432 | bytes 18059356 | solution.py:31
  112.6 23.0 %multiply_convert_fusion.6 = bf16[8192,512]{0,1:T(8,128)(2,1)S(1)} fusion(f32[16,8192]{1,0:T(8,128)S(1)} %get-tuple-element.462, f32[512]{0:T(512)S(1)} %multiply_reduce_fusion.7, f32[8192]{0:T(1024)S(1)} %get-tuple-element.460, f32[1,16,512]{2,0,1:T(1,128)S(1)} %constant_dynamic-slice_fusion.6), kind=kOutput, calls=%fused_computation.12.clone.1 | convolution fusion | flops 843055104 | bytes 8980480 | tf_op jit(solution)/shard_map/while/body/eval_jaxpr/dot_general | solution.py:11
  138.3 23.0 %multiply_convert_fusion.6 = bf16[8192,512]{0,1:T(8,128)(2,1)S(1)} fusion(f32[16,8192]{1,0:T(8,128)S(1)} %get-tuple-element.462, f32[512]{0:T(512)S(1)} %multiply_reduce_fusion.7, f32[8192]{0:T(1024)S(1)} %get-tuple-element.460, f32[1,16,512]{2,0,1:T(1,128)S(1)} %constant_dynamic-slice_fusion.6), kind=kOutput, calls=%fused_computation.12.clone.1 | convolution fusion | flops 843055104 | bytes 8980480 | tf_op jit(solution)/shard_map/while/body/eval_jaxpr/dot_general | solution.py:11
  164.0 23.0 %multiply_convert_fusion.6 = bf16[8192,512]{0,1:T(8,128)(2,1)S(1)} fusion(f32[16,8192]{1,0:T(8,128)S(1)} %get-tuple-element.462, f32[512]{0:T(512)S(1)} %multiply_reduce_fusion.7, f32[8192]{0:T(1024)S(1)} %get-tuple-element.460, f32[1,16,512]{2,0,1:T(1,128)S(1)} %constant_dynamic-slice_fusion.6), kind=kOutput, calls=%fused_computation.12.clone.1 | convolution fusion | flops 843055104 | bytes 8980480 | tf_op jit(solution)/shard_map/while/body/eval_jaxpr/dot_general | solution.py:11
  189.7 23.0 %multiply_convert_fusion.6 = bf16[8192,512]{0,1:T(8,128)(2,1)S(1)} fusion(f32[16,8192]{1,0:T(8,128)S(1)} %get-tuple-element.462, f32[512]{0:T(512)S(1)} %multiply_reduce_fusion.7, f32[8192]{0:T(1024)S(1)} %get-tuple-element.460, f32[1,16,512]{2,0,1:T(1,128)S(1)} %constant_dynamic-slice_fusion.6), kind=kOutput, calls=%fused_computation.12.clone.1 | convolution fusion | flops 843055104 | bytes 8980480 | tf_op jit(solution)/shard_map/while/body/eval_jaxpr/dot_general | solution.py:11
  218.3 11.6 %all-reduce.6.cloned.1.call-start = ((), (), s32[]{:S(2)}) async-start(), calls=%async_computation.2 | async-start | bytes 2097152 | tf_op jit(solution)/shard_map/psum | solution.py:59
  229.9 9.8 gather_fusion.5
  250.1 114.9 %all-reduce.4.cloned.1.call-done = f32[32,2048]{0,1:T(8,128)} async-done(((f32[32,2048]{0,1:T(8,128)}), f32[32,2048]{0,1:T(8,128)}) %all-reduce.4.cloned.1.call-update) | async-done | bytes 262160 | tf_op jit(solution)/shard_map/psum | solution.py:59
  364.9 15.7 %scatter_custom_fusion = f32[32,8192]{0,1:T(8,128)} fusion(s32[2048]{0:T(1024)S(1)} %bitcast.192, f32[]{:T(128)} %constant.139.clone.1, f32[32,2048]{0,1:T(8,128)} %all-reduce.4.cloned.1.call-done, f32[2048]{0:T(1024)S(1)} %bitcast.186), kind=kCustom, calls=%fused_computation.42 | custom fusion | flops 131072 | bytes 1318916 | tf_op jit(solution)/shard_map/scatter-add | solution.py:60
  389.0 102.9 %while.37 = (s32[]{:T(128)}, f32[4,32,512]{2,1,0:T(8,128)S(1)}, f32[8192]{0:T(1024)S(1)}, f32[4,16,512]{2,0,1:T(4,128)S(1)}, f32[16,8192]{1,0:T(8,128)S(1)}, /*index=5*/bf16[32,8192]{1,0:T(8,128)(2,1)S(1)}, s32[]{:T(128)}) while((s32[]{:T(128)}, f32[4,32,512]{2,1,0:T(8,128)S(1)}, f32[8192]{0:T(1024)S(1)}, f32[4,16,512]{2,0,1:T(4,128)S(1)}, ...), condition=%wide.region_10.13_spmd, body=%wide.region_8.12_spmd.sunk | while | flops 1111506432 | bytes 18059356 | solution.py:31
  389.1 23.0 %multiply_convert_fusion.7 = bf16[8192,512]{0,1:T(8,128)(2,1)S(1)} fusion(f32[16,8192]{1,0:T(8,128)S(1)} %get-tuple-element.483, f32[512]{0:T(512)S(1)} %multiply_reduce_fusion.8, f32[8192]{0:T(1024)S(1)} %get-tuple-element.481, f32[1,16,512]{2,0,1:T(1,128)S(1)} %constant_dynamic-slice_fusion.7), kind=kOutput, calls=%fused_computation.22.clone.1 | convolution fusion | flops 843055104 | bytes 8980480 | tf_op jit(solution)/shard_map/while/body/eval_jaxpr/dot_general | solution.py:11
  414.8 23.0 %multiply_convert_fusion.7 = bf16[8192,512]{0,1:T(8,128)(2,1)S(1)} fusion(f32[16,8192]{1,0:T(8,128)S(1)} %get-tuple-element.483, f32[512]{0:T(512)S(1)} %multiply_reduce_fusion.8, f32[8192]{0:T(1024)S(1)} %get-tuple-element.481, f32[1,16,512]{2,0,1:T(1,128)S(1)} %constant_dynamic-slice_fusion.7), kind=kOutput, calls=%fused_computation.22.clone.1 | convolution fusion | flops 843055104 | bytes 8980480 | tf_op jit(solution)/shard_map/while/body/eval_jaxpr/dot_general | solution.py:11
  440.5 23.0 %multiply_convert_fusion.7 = bf16[8192,512]{0,1:T(8,128)(2,1)S(1)} fusion(f32[16,8192]{1,0:T(8,128)S(1)} %get-tuple-element.483, f32[512]{0:T(512)S(1)} %multiply_reduce_fusion.8, f32[8192]{0:T(1024)S(1)} %get-tuple-element.481, f32[1,16,512]{2,0,1:T(1,128)S(1)} %constant_dynamic-slice_fusion.7), kind=kOutput, calls=%fused_computation.22.clone.1 | convolution fusion | flops 843055104 | bytes 8980480 | tf_op jit(solution)/shard_map/while/body/eval_jaxpr/dot_general | solution.py:11
  466.2 23.0 %multiply_convert_fusion.7 = bf16[8192,512]{0,1:T(8,128)(2,1)S(1)} fusion(f32[16,8192]{1,0:T(8,128)S(1)} %get-tuple-element.483, f32[512]{0:T(512)S(1)} %multiply_reduce_fusion.8, f32[8192]{0:T(1024)S(1)} %get-tuple-element.481, f32[1,16,512]{2,0,1:T(1,128)S(1)} %constant_dynamic-slice_fusion.7), kind=kOutput, calls=%fused_computation.22.clone.1 | convolution fusion | flops 843055104 | bytes 8980480 | tf_op jit(solution)/shard_map/while/body/eval_jaxpr/dot_general | solution.py:11
  492.2 9.8 gather_fusion.4
  504.7 9.6 all_gather.19
  514.4 138.7 %all-reduce.6.cloned.1.call-done = f32[32,2048]{0,1:T(8,128)} async-done(((f32[32,2048]{0,1:T(8,128)}), f32[32,2048]{0,1:T(8,128)}) %all-reduce.6.cloned.1.call-update) | async-done | bytes 262160 | tf_op jit(solution)/shard_map/psum | solution.py:59
  653.2 15.7 %scatter_custom_fusion.1 = f32[32,8192]{0,1:T(8,128)} fusion(s32[2048]{0:T(1024)} %bitcast.191, f32[]{:T(128)} %constant.139.clone.1, f32[32,2048]{0,1:T(8,128)} %all-reduce.6.cloned.1.call-done, f32[2048]{0:T(1024)S(1)} %bitcast.183), kind=kCustom, calls=%fused_computation.40 | custom fusion | flops 131072 | bytes 2105856 | tf_op jit(solution)/shard_map/scatter-add | solution.py:60
  668.8 10.3 %fusion.29 = (bf16[32,8192]{0,1:T(8,128)(2,1)S(1)}, f32[32,8192]{0,1:T(8,128)}, f32[32,8192]{0,1:T(8,128)}) fusion(f32[32,8192]{0,1:T(8,128)} %get-tuple-element.324, f32[32,8192]{0,1:T(8,128)} %scatter_custom_fusion.1, f32[32,8192]{0,1:T(8,128)} %scatter_custom_fusion, f32[32,8192]{0,1:T(8,128)} %copy.61), kind=kLoop, calls=%fused_computation.76 | loop fusion | flops 2097152 | bytes 6815744 | tf_op jit(solution)/shard_map/convert_element_type | solution.py:63
  680.0 210.8 %while.38 = (s32[]{:T(128)}, f32[8,32,512]{2,1,0:T(8,128)}, f32[8192]{0:T(1024)S(1)}, f32[8,16,512]{2,0,1:T(8,128)S(1)}, f32[16,8192]{1,0:T(8,128)S(1)}, /*index=5*/bf16[32,8192]{1,0:T(8,128)(2,1)S(1)}, s32[]{:T(128)}) while((s32[]{:T(128)}, f32[8,32,512]{2,1,0:T(8,128)}, f32[8192]{0:T(1024)S(1)}, f32[8,16,512]{2,0,1:T(8,128)S(1)}, ...), condition=%wide.region_15.18_spmd, body=%wide.region_13.17_spmd.sunk | while | flops 1111506432 | bytes 18059356 | solution.py:31
  680.0 23.0 %multiply_convert_fusion.8 = bf16[8192,512]{0,1:T(8,128)(2,1)S(1)} fusion(f32[16,8192]{1,0:T(8,128)S(1)} %get-tuple-element.504, f32[512]{0:T(512)S(1)} %multiply_reduce_fusion.9, f32[8192]{0:T(1024)S(1)} %get-tuple-element.502, f32[1,16,512]{2,0,1:T(1,128)S(1)} %constant_dynamic-slice_fusion.8), kind=kOutput, calls=%fused_computation.32.clone.1 | convolution fusion | flops 843055104 | bytes 8980480 | tf_op jit(solution)/shard_map/while/body/eval_jaxpr/dot_general | solution.py:11
  706.4 23.0 %multiply_convert_fusion.8 = bf16[8192,512]{0,1:T(8,128)(2,1)S(1)} fusion(f32[16,8192]{1,0:T(8,128)S(1)} %get-tuple-element.504, f32[512]{0:T(512)S(1)} %multiply_reduce_fusion.9, f32[8192]{0:T(1024)S(1)} %get-tuple-element.502, f32[1,16,512]{2,0,1:T(1,128)S(1)} %constant_dynamic-slice_fusion.8), kind=kOutput, calls=%fused_computation.32.clone.1 | convolution fusion | flops 843055104 | bytes 8980480 | tf_op jit(solution)/shard_map/while/body/eval_jaxpr/dot_general | solution.py:11
  732.7 23.0 %multiply_convert_fusion.8 = bf16[8192,512]{0,1:T(8,128)(2,1)S(1)} fusion(f32[16,8192]{1,0:T(8,128)S(1)} %get-tuple-element.504, f32[512]{0:T(512)S(1)} %multiply_reduce_fusion.9, f32[8192]{0:T(1024)S(1)} %get-tuple-element.502, f32[1,16,512]{2,0,1:T(1,128)S(1)} %constant_dynamic-slice_fusion.8), kind=kOutput, calls=%fused_computation.32.clone.1 | convolution fusion | flops 843055104 | bytes 8980480 | tf_op jit(solution)/shard_map/while/body/eval_jaxpr/dot_general | solution.py:11
  759.1 23.0 %multiply_convert_fusion.8 = bf16[8192,512]{0,1:T(8,128)(2,1)S(1)} fusion(f32[16,8192]{1,0:T(8,128)S(1)} %get-tuple-element.504, f32[512]{0:T(512)S(1)} %multiply_reduce_fusion.9, f32[8192]{0:T(1024)S(1)} %get-tuple-element.502, f32[1,16,512]{2,0,1:T(1,128)S(1)} %constant_dynamic-slice_fusion.8), kind=kOutput, calls=%fused_computation.32.clone.1 | convolution fusion | flops 843055104 | bytes 8980480 | tf_op jit(solution)/shard_map/while/body/eval_jaxpr/dot_general | solution.py:11
  785.4 23.0 %multiply_convert_fusion.8 = bf16[8192,512]{0,1:T(8,128)(2,1)S(1)} fusion(f32[16,8192]{1,0:T(8,128)S(1)} %get-tuple-element.504, f32[512]{0:T(512)S(1)} %multiply_reduce_fusion.9, f32[8192]{0:T(1024)S(1)} %get-tuple-element.502, f32[1,16,512]{2,0,1:T(1,128)S(1)} %constant_dynamic-slice_fusion.8), kind=kOutput, calls=%fused_computation.32.clone.1 | convolution fusion | flops 843055104 | bytes 8980480 | tf_op jit(solution)/shard_map/while/body/eval_jaxpr/dot_general | solution.py:11
  811.8 23.0 %multiply_convert_fusion.8 = bf16[8192,512]{0,1:T(8,128)(2,1)S(1)} fusion(f32[16,8192]{1,0:T(8,128)S(1)} %get-tuple-element.504, f32[512]{0:T(512)S(1)} %multiply_reduce_fusion.9, f32[8192]{0:T(1024)S(1)} %get-tuple-element.502, f32[1,16,512]{2,0,1:T(1,128)S(1)} %constant_dynamic-slice_fusion.8), kind=kOutput, calls=%fused_computation.32.clone.1 | convolution fusion | flops 843055104 | bytes 8980480 | tf_op jit(solution)/shard_map/while/body/eval_jaxpr/dot_general | solution.py:11
  838.1 23.0 %multiply_convert_fusion.8 = bf16[8192,512]{0,1:T(8,128)(2,1)S(1)} fusion(f32[16,8192]{1,0:T(8,128)S(1)} %get-tuple-element.504, f32[512]{0:T(512)S(1)} %multiply_reduce_fusion.9, f32[8192]{0:T(1024)S(1)} %get-tuple-element.502, f32[1,16,512]{2,0,1:T(1,128)S(1)} %constant_dynamic-slice_fusion.8), kind=kOutput, calls=%fused_computation.32.clone.1 | convolution fusion | flops 843055104 | bytes 8980480 | tf_op jit(solution)/shard_map/while/body/eval_jaxpr/dot_general | solution.py:11
  864.4 23.0 %multiply_convert_fusion.8 = bf16[8192,512]{0,1:T(8,128)(2,1)S(1)} fusion(f32[16,8192]{1,0:T(8,128)S(1)} %get-tuple-element.504, f32[512]{0:T(512)S(1)} %multiply_reduce_fusion.9, f32[8192]{0:T(1024)S(1)} %get-tuple-element.502, f32[1,16,512]{2,0,1:T(1,128)S(1)} %constant_dynamic-slice_fusion.8), kind=kOutput, calls=%fused_computation.32.clone.1 | convolution fusion | flops 843055104 | bytes 8980480 | tf_op jit(solution)/shard_map/while/body/eval_jaxpr/dot_general | solution.py:11
  892.7 20.9 %reduce-scatter.2.cloned.1.call-done = f32[32,1024]{1,0:T(8,128)} async-done(((f32[32,4096]{1,0:T(8,128)}), f32[32,1024]{1,0:T(8,128)}) %reduce-scatter.2.cloned.1.call-update) | async-done | bytes 131088 | tf_op jit(solution)/shard_map/reduce_scatter | solution.py:67
  920.8 97.2 %all-reduce.8.cloned.1.call-done = f32[32,1024]{1,0:T(8,128)} async-done(((f32[32,1024]{1,0:T(8,128)}), f32[32,1024]{1,0:T(8,128)}) %all-reduce.8.cloned.1.call-update) | async-done | bytes 131088 | tf_op jit(solution)/shard_map/psum | solution.py:68
  (114 shorter events, 128.0 us)
Async XLA Ops:
  7.2 23.3 %copy-start = (f32[32,8192]{1,0:T(8,128)S(1)}, f32[32,8192]{1,0:T(8,128)}, u32[]{:S(2)}) copy-start(f32[32,8192]{1,0:T(8,128)} %param.17) | copy-start | bytes 3145732
  7.2 98.6 %all-gather.5.cloned.1.call-start = ((), (), s32[]{:S(2)}) async-start(), calls=%async_computation.5 | async-start | bytes 16908288 | tf_op jit(solution)/shard_map/all_gather | solution.py:53
  8.1 25.2 %copy-start.3 = (f32[1,2048]{1,0:T(1,128)}, f32[1,2048]{1,0:T(1,128)S(1)}, u32[]{:S(2)}) copy-start(f32[1,2048]{1,0:T(1,128)S(1)} %get-tuple-element.329) | copy-start | bytes 24580
  21.7 221.6 %all-gather.7.cloned.1.call-start = ((), (), s32[]{:S(2)}) async-start(), calls=%async_computation.6 | async-start | bytes 16908288 | tf_op jit(solution)/shard_map/all_gather | solution.py:53
  29.7 24.7 %copy-start.6 = (pred[2048]{0:T(1024)(128)(4,1)}, pred[2048]{0:T(1024)(128)(4,1)S(1)}, u32[]{:S(2)}) copy-start(pred[2048]{0:T(1024)(128)(4,1)S(1)} %compare_and_fusion) | copy-start | bytes 6148
  30.4 24.0 %copy-start.1 = (f32[16,8192]{1,0:T(8,128)S(1)}, f32[16,8192]{1,0:T(8,128)}, u32[]{:S(2)}) copy-start(f32[16,8192]{1,0:T(8,128)} %param.16) | copy-start | bytes 1572868
  30.4 334.5 %all-reduce.4.cloned.1.call-start = ((), (), s32[]{:S(2)}) async-start(), calls=%async_computation.1 | async-start | bytes 2097152 | tf_op jit(solution)/shard_map/psum | solution.py:59
  218.3 434.8 %all-reduce.6.cloned.1.call-start = ((), (), s32[]{:S(2)}) async-start(), calls=%async_computation.2 | async-start | bytes 2097152 | tf_op jit(solution)/shard_map/psum | solution.py:59
  389.0 113.1 %copy-start.2 = (f32[2048,32]{1,0:T(8,128)S(1)}, f32[2048,32]{1,0:T(8,128)}, u32[]{:S(2)}) copy-start(f32[2048,32]{1,0:T(8,128)} %gather_fusion.5) | copy-start | bytes 786436
  389.0 113.1 %copy-start.4 = (f32[1,2048]{1,0:T(1,128)S(1)}, f32[1,2048]{1,0:T(1,128)}, u32[]{:S(2)}) copy-start(f32[1,2048]{1,0:T(1,128)} %copy-done.3) | copy-start | bytes 24580
  389.0 113.1 %copy-start.7 = (pred[2048]{0:T(1024)(128)(4,1)S(1)}, pred[2048]{0:T(1024)(128)(4,1)}, u32[]{:S(2)}) copy-start(pred[2048]{0:T(1024)(128)(4,1)} %copy-done.6) | copy-start | bytes 6148
  491.9 12.9 %copy-start.5 = (f32[16,1024]{1,0:T(8,128)S(1)}, f32[16,1024]{1,0:T(8,128)}, u32[]{:S(2)}) copy-start(f32[16,1024]{1,0:T(8,128)} %param.21) | copy-start | bytes 196612
  504.7 408.9 %reduce-scatter.2.cloned.1.call-start = ((), (), s32[]{:S(2)}) async-start(), calls=%async_computation.3 | async-start | bytes 655360 | tf_op jit(solution)/shard_map/reduce_scatter | solution.py:67
  892.6 125.4 %all-reduce.8.cloned.1.call-start = ((), (), s32[]{:S(2)}) async-start(), calls=%async_computation.4 | async-start | bytes 262144 | tf_op jit(solution)/shard_map/psum | solution.py:68
Sparse Core Ops, SparseCore 0:
  21.8 83.9 all-gather.4
  109.0 79.8 all-gather.6
  218.5 146.4 all-reduce.3
  504.8 148.3 all-reduce.5
  892.8 20.7 reduce-scatter.1
  916.7 101.3 all-reduce.7
